TPU v7x, 256 devices: a whole 4x4x8 slice. The times are simulated.
256 devices in a mesh: ha: 16 (over x, z_lo), wa: 16 (over z_hi, y, core).
Axes of the slice: x: 4, y: 4, z: 8 (z_hi: 2, z_lo: 4; z = z_hi * 4 + z_lo), core: 2. Of those that a mesh axis runs over, the one named last changes fastest.
Arguments:
- features: bfloat16 [4, 128, 512, 256], P(None, 'ha', 'wa'), may hold values from -6 to 6
- weights: bfloat16 [3, 3, 3, 256, 256], replicated, may hold values from -0.078125 to 0.078125
- cotangent: bfloat16 [4, 128, 512, 256], P(None, 'ha', 'wa'), may hold values from -6 to 6
Outputs:
- block_out: bfloat16 [4, 128, 512, 256], P(None, 'ha', 'wa')
- feature_grad: bfloat16 [4, 128, 512, 256], P(None, 'ha', 'wa')
- weight_grad: float32 [27, 256, 256], P(None, 'ha', 'wa')
All inputs are finite; a program needn't handle non-finite values.
Results may differ from a plain program's by a relative error of at most 0.0032.
Values may be sent and summed in bfloat16 or wider, within the bound.
A program may use at most 256 MiB of HBM per device.

v0:
```python
import jax
import jax.numpy as jnp
from jax import lax
from jax.experimental import pallas as pl
from jax.experimental.pallas import tpu as pltpu
from jax.sharding import PartitionSpec as P

MESH = pl.DeviceIdType.MESH
BF, F32 = jnp.bfloat16, jnp.float32
PAIRS = 14
FOLD = (((0, 4),), ((0, 3), (1, 2)), ((0, 0), (1, 1), (2, 2)), ((1, 0), (2, 1), (3, 2)))


def mm(a, b):
    return jnp.dot(a, b, preferred_element_type=F32)


def nt(a, b):
    return lax.dot_general(a, b, (((1,), (1,)), ((), ())), preferred_element_type=F32)


def iota(shape, dim):
    return lax.broadcasted_iota(jnp.int32, shape, dim)


def kernel(
    feat_hbm, w_hbm, cot_hbm,
    bo_hbm, fg_hbm, wg_ref,
    w_ref, wsum, tile, gtile, xc, xc2, xg, cot, bo, fg, acc_ref, fix_ref, hold, gt, gt2,
    cols, gcols, left, right, gleft, gright,
    part, partb, r1, s1, s1b, r2, s2, of, ob, r3,
    local_sem, hs, hr, ghs, ghr, xcs, xcr, gts, gtr, s1s, s1r, s2s, s2r, s3s, s3r,
):
    ha, wa = lax.axis_index("ha"), lax.axis_index("wa")
    x, zlo = ha // 4, ha % 4
    zhi, y, core = wa // 8, (wa // 2) % 4, wa % 2
    z = zhi * 4 + zlo

    def device(dx=0, dy=0, dz=0, dc=0):
        nx, ny, nz, nc = (x + dx) % 4, (y + dy) % 4, (z + dz) % 8, (core + dc) % 2
        return (nx * 4 + nz % 4, (nz // 4) * 8 + ny * 2 + nc)

    other = device(dc=1)
    north, south, west, east = ha > 0, ha < 15, wa > 0, wa < 15
    sides = (
        (north, -1, 0), (south, 1, 0), (west, 0, -1), (east, 0, 1),
        (north & west, -1, -1), (north & east, -1, 1), (south & west, 1, -1), (south & east, 1, 1),
    )

    loads = [
        pltpu.make_async_copy(feat_hbm, tile.at[:, 1:9, 16:48, :], local_sem.at[0]),
        pltpu.make_async_copy(w_hbm, w_ref, local_sem.at[1]),
        pltpu.make_async_copy(cot_hbm, cot, local_sem.at[2]),
    ]
    for copy in loads:
        copy.start()

    barrier = pltpu.get_barrier_semaphore()
    count = 14
    for present, dr, dc in sides:
        @pl.when(present)
        def _():
            pl.semaphore_signal(barrier, inc=1, device_id=(ha + dr, wa + dc), device_id_type=MESH)
        count = count + present.astype(jnp.int32)
    peers = [device(dy=d) for d in (1, 2, 3)] + [device(dx=d) for d in (1, 2, 3)]
    peers += [device(dz=d) for d in range(1, 8)] + [other]
    for peer in peers:
        pl.semaphore_signal(barrier, inc=1, device_id=peer, device_id_type=MESH)

    m, n = iota((128, 1024), 0), iota((128, 1024), 1)
    column = jnp.where(m < 64, 31, 0)
    place = m % 64
    pick = jnp.where(place < 32, place * 32, jnp.where(place < 48, (place - 32) * 256, (place - 48) * 256 + 224)) + column
    select = jnp.where(pick == n, 1.0, 0.0).astype(BF)
    m, n = iota((512, 32), 0), iota((512, 32), 1)
    spread = jnp.where(m // 16 == n, 1.0, 0.0).astype(BF)
    m, n = iota((128, 32), 0), iota((128, 32), 1)
    corner = jnp.where(m // 64 * 16 + (m % 64) // 16 == n, 1.0, 0.0).astype(BF)

    def halo_copies(padded, packed, lhs, rhs, send, recv):
        row_src = {-1: padded.at[:, 1, 16:48, :], 1: padded.at[:, 8, 16:48, :]}
        row_dst = {-1: padded.at[:, 9, 16:48, :], 1: padded.at[:, 0, 16:48, :]}
        copies = []
        for i, (present, dr, dc) in enumerate(sides):
            if dc == 0:
                src, dst = row_src[dr], row_dst[dr]
            else:
                base = 0 if dc == 1 else 64
                target = lhs if dc == 1 else rhs
                if dr == 0:
                    src, dst = packed.at[base:base + 32], target.at[0:32]
                elif dr == -1:
                    src, dst = packed.at[base + 32:base + 48], target.at[48:64]
                else:
                    src, dst = packed.at[base + 48:base + 64], target.at[32:48]
            back = {(-1, 0): 1, (1, 0): 0, (0, -1): 3, (0, 1): 2, (-1, -1): 7, (-1, 1): 6, (1, -1): 5, (1, 1): 4}[(dr, dc)]
            copies.append((present, pltpu.make_async_remote_copy(
                src_ref=src, dst_ref=dst, send_sem=send.at[i], recv_sem=recv.at[back],
                device_id=(ha + dr, wa + dc), device_id_type=MESH)))
        return copies

    def halo_wait(padded, lhs, rhs, recv, which):
        landing = (
            padded.at[:, 0, 16:48, :], padded.at[:, 9, 16:48, :], lhs.at[0:32], rhs.at[0:32],
            lhs.at[32:48], rhs.at[32:48], lhs.at[48:64], rhs.at[48:64],
        )
        for i in which:
            present, ref = sides[i][0], landing[i]

            @pl.when(present)
            def _():
                pltpu.make_async_copy(ref, ref, recv.at[i]).wait()

            @pl.when(jnp.logical_not(present))
            def _():
                ref[...] = jnp.zeros(ref.shape, BF)

    def shifted(padded, lhs, rhs, out, rows, centre):
        if 1 in rows:
            padded[:, 1:9, 0:16, :] = mm(spread, lhs[0:32]).astype(BF).reshape(4, 8, 16, 256)
            padded[:, 1:9, 48:64, :] = mm(spread, rhs[0:32]).astype(BF).reshape(4, 8, 16, 256)
        if 0 in rows:
            for side, lanes in ((lhs, slice(0, 16)), (rhs, slice(48, 64))):
                ends = mm(corner, side[32:64]).astype(BF).reshape(2, 4, 16, 256)
                padded[:, 0, lanes, :] = ends[0]
                padded[:, 9, lanes, :] = ends[1]
        for t in range(4):
            for r in rows:
                for c in range(3):
                    if c != 1 or centre:
                        out[c, t, r * 32:r * 32 + 32, :] = padded[t, r, 15 + c:47 + c, :]

    middle, ends = tuple(range(1, 9)), (0, 9)

    zero_rows = jnp.zeros((32, 256), BF)
    for c in range(3):
        for t in range(4):
            for r in ends:
                xc[c, t, r * 32:r * 32 + 32, :] = zero_rows
    loads[0].wait()
    cols[...] = mm(select, tile[:, 1:9, 16:48, :].reshape(1024, 256)).astype(BF)
    pl.semaphore_wait(barrier, count)
    halo = halo_copies(tile, cols, left, right, hs, hr)
    for i in (2, 3, 0, 1, 4, 5, 6, 7):
        pl.when(halo[i][0])(halo[i][1].start)
    for t in range(4):
        for r in middle:
            xc[1, t, r * 32:r * 32 + 32, :] = tile[t, r, 16:48, :]

    def x_copy(i):
        ref = (lambda b: (b.at[1, :, 32:288], b.at[0, :, 32:288], b.at[2, :, 32:288], b.at[:, :, 0:32], b.at[:, :, 288:320])[i])
        return pltpu.make_async_remote_copy(
            src_ref=ref(xc), dst_ref=ref(xc2), send_sem=xcs.at[i], recv_sem=xcr.at[i], device_id=other, device_id_type=MESH)

    x_copy(0).start()
    loads[1].wait()

    def forward(t, columns):
        total = None
        for f, a in FOLD[t]:
            for b in range(3):
                for c in columns:
                    lanes = slice(c * 256, c * 256 + 256)
                    weight = w_ref[a * 3 + b, lanes] if a < 3 else wsum[(a - 3) * 3 + b, lanes]
                    term = mm(xc[c, f, b * 32:b * 32 + 256, :], weight)
                    total = term if total is None else total + term
        return total

    for t in (3, 2):
        acc_ref[t] = forward(t, (1,))
    for b in range(3):
        two = w_ref[b].astype(F32) + w_ref[3 + b].astype(F32)
        wsum[b] = two.astype(BF)
        wsum[3 + b] = (two + w_ref[6 + b].astype(F32)).astype(BF)
    for t in (1, 0):
        acc_ref[t] = forward(t, (1,))
    halo_wait(tile, left, right, hr, (2, 3))
    shifted(tile, left, right, xc, middle, False)
    x_copy(1).start()
    x_copy(2).start()
    for t in range(4):
        acc_ref[t] += forward(t, (0, 2))
    halo_wait(tile, left, right, hr, (0, 1, 4, 5, 6, 7))
    shifted(tile, left, right, xc, ends, True)
    x_copy(3).start()
    x_copy(4).start()
    for side, (lo, b) in enumerate(((0, 0), (288, 2))):
        total = None
        for a in range(3):
            for c in range(3):
                rows = jnp.concatenate([xc[c, max(t + a - 2, 0), lo:lo + 32, :] for t in range(4)], axis=0)
                term = mm(rows, w_ref[a * 3 + b, c * 256:c * 256 + 256])
                total = term if total is None else total + term
        fix_ref[side] = total
    loads[2].wait()

    def g_copy(t):
        return pltpu.make_async_remote_copy(
            src_ref=gt.at[:, 1 - core, :, t * 256:t * 256 + 256], dst_ref=gt2.at[:, :, t * 256:t * 256 + 256],
            send_sem=gts.at[t], recv_sem=gtr.at[t], device_id=other, device_id_type=MESH)

    for t in range(4):
        acc_ref[t, 0:32] += fix_ref[0, t * 32:t * 32 + 32]
        acc_ref[t, 224:256] += fix_ref[1, t * 32:t * 32 + 32]
        acc = acc_ref[t]
        logistic = jax.nn.sigmoid(acc)
        own = tile[t, 1:9, 16:48, :].reshape(256, 256).astype(F32)
        bo[t] = (own + acc * logistic).astype(BF).reshape(8, 32, 256)
        grad = cot[t].reshape(256, 256).astype(F32) * logistic * (1.0 + acc * (1.0 - logistic))
        grad = grad.astype(BF)
        gtile[t, 1:9, 16:48, :] = grad.reshape(8, 32, 256)
        gt[:, :, :, t * 256:t * 256 + 256] = grad.T.reshape(8, 2, 16, 256)
        g_copy(t).start()

    low = iota((128, 128), 1) < 64

    def tap_term(tap, both):
        a, b, c = tap // 9, (tap // 3) % 3, tap % 3
        total = None
        for mine in both:
            for t in range(4):
                lanes = slice(t * 256, t * 256 + 256)
                one = gt[:, core, :, lanes] if mine else gt2[:, :, lanes]
                window = (xc if mine else xc2)[c, max(t + a - 2, 0), b * 32:b * 32 + 256, :]
                term = mm(one.reshape(128, 256), window)
                total = term if total is None else total + term
        return total

    def store_pair(p, by_y):
        for half in range(2):
            lanes = slice(half * 128, half * 128 + 128)
            one, two = hold[p % 4, 0, :, lanes], hold[p % 4, 1, :, lanes]
            both = (jnp.where(low, one, pltpu.roll(two, 64, 1)), jnp.where(low, pltpu.roll(one, 64, 1), two))
            for k, block in enumerate(both):
                for zz in range(2):
                    for yy in range(4):
                        rows = block[(zz * 4 + yy) * 16:(zz * 4 + yy) * 16 + 16]
                        i, j = (yy, 2 * half + k) if by_y else (2 * half + k, yy)
                        part[p, i, j, zz * 16:zz * 16 + 16] = rows
                        partb[p, i, j, zz * 16:zz * 16 + 16] = rows.astype(BF)

    def first_copy(p, d, by_y):
        return pltpu.make_async_remote_copy(
            src_ref=partb.at[p, ((y if by_y else x) + d) % 4], dst_ref=r1.at[p, d - 1],
            send_sem=s1s.at[p, d - 1], recv_sem=s1r.at[p, d - 1],
            device_id=device(dy=d) if by_y else device(dx=d), device_id_type=MESH)

    def second_copy(p, d, by_y):
        return pltpu.make_async_remote_copy(
            src_ref=s1b.at[p, ((y if by_y else x) + d) % 4], dst_ref=r2.at[p, d - 1],
            send_sem=s2s.at[p, d - 1], recv_sem=s2r.at[p, d - 1],
            device_id=device(dy=d) if by_y else device(dx=d), device_id_type=MESH)

    def third_copy(q, d):
        nz = (z + d) % 8
        return pltpu.make_async_remote_copy(
            src_ref=ob.at[nz % 4, nz // 4, q], dst_ref=r3.at[q, d - 1], send_sem=s3s.at[q, d - 1], recv_sem=s3r.at[q, d - 1],
            device_id=device(dz=d), device_id_type=MESH)

    def over_pairs(q, body):
        @pl.loop(2 * q, min(2 * q + 2, PAIRS // 2))
        def _(i):
            for k in range(2):
                body(2 * i + k, k == 0)

    def own_terms(pairs):
        for p in pairs:
            for i in range(2):
                hold[p, i] = tap_term(2 * p + i, (True,))

    def pair_terms(p):
        for i in range(2):
            tap = min(2 * p + i, 26)
            hold[p % 4, i] = hold[p, i] + tap_term(tap, (False,)) if p < 4 else tap_term(tap, (True, False))

    def weight_group(done, new):
        for p in new:
            pair_terms(p)
        for p in done:
            store_pair(p, p % 2 == 0)
        for p in done:
            for d in (2, 1, 3):
                first_copy(p, d, p % 2 == 0).start()

    def first_sum(q):
        def body(p, by_y):
            for d in (1, 2, 3):
                first_copy(p, d, by_y).wait_recv()
            total = part[p, y if by_y else x]
            for d in range(3):
                total = total + r1[p, d].astype(F32)
            s1[p] = total
            s1b[p] = total.astype(BF)
            for d in (2, 1, 3):
                second_copy(p, d, not by_y).start()
        over_pairs(q, body)

    lane = iota((32, 128), 1)

    def exchange(one, two, width):
        lower = (lane // width) % 2 == 0
        return (jnp.where(lower, one, pltpu.roll(two, width, 1)),
                jnp.where(lower, pltpu.roll(one, 128 - width, 1), two))

    def second_sum(q):
        def body(p, by_y):
            for d in (1, 2, 3):
                second_copy(p, d, not by_y).wait_recv()
            total = s1[p, x if by_y else y]
            for d in range(3):
                total = total + r2[p, d].astype(F32)
            s2[p] = total
        over_pairs(q, body)
        v = [s2[4 * q + i] if 4 * q + i < PAIRS else jnp.zeros((32, 128), F32) for i in range(4)]
        v[0], v[1] = exchange(v[0], v[1], 16)
        v[2], v[3] = exchange(v[2], v[3], 16)
        v[0], v[2] = exchange(v[0], v[2], 32)
        v[1], v[3] = exchange(v[1], v[3], 32)
        for i in range(4):
            for zz in range(2):
                of[i, zz, q] = v[i][zz * 16:zz * 16 + 16]
                ob[i, zz, q] = v[i][zz * 16:zz * 16 + 16].astype(BF)
        for d in (4, 3, 5, 2, 6, 1, 7):
            third_copy(q, d).start()

    def feature_gradient(frames):
        jobs = {}
        for t in frames:
            terms = [(t + 2 - a, a) for a in range(3) if t + 2 - a < 4] if t else [(2, 0), (1, 3), (0, 4)]
            jobs[t] = [(f, a, b, c) for f, a in terms for b in range(3) for c in range(3)]
        totals = dict.fromkeys(frames)
        for i in range(max(len(job) for job in jobs.values())):
            for t in frames:
                if i < len(jobs[t]):
                    f, a, b, c = jobs[t][i]
                    index = a * 3 + 2 - b if a < 3 else (a - 3) * 3 + 2 - b
                    weight = (w_ref if a < 3 else wsum)[index, (2 - c) * 256:(2 - c) * 256 + 256, :]
                    term = nt(xg[c, f, b * 32:b * 32 + 256, :], weight)
                    totals[t] = term if totals[t] is None else totals[t] + term
        for t in frames:
            total = totals[t] + cot[t].reshape(256, 256).astype(F32)
            fg[t] = total.astype(BF).reshape(8, 32, 256)

    ghalo = halo_copies(gtile, gcols, gleft, gright, ghs, ghr)
    for i in (0, 1):
        pl.when(ghalo[i][0])(ghalo[i][1].start)
    own_terms(range(4))
    for t in range(4):
        g_copy(t).wait_recv()
    for i in range(5):
        x_copy(i).wait_recv()
    weight_group((), (0,))
    weight_group((0,), (1,))
    weight_group((1,), (2, 3))
    gcols[...] = mm(select, gtile[:, 1:9, 16:48, :].reshape(1024, 256)).astype(BF)
    for i in range(2, 8):
        pl.when(ghalo[i][0])(ghalo[i][1].start)
    weight_group((2, 3), (4, 5))
    weight_group((4, 5), (6, 7))
    weight_group((6, 7), (8, 9))
    weight_group((8, 9), (10, 11))
    bo_out = pltpu.make_async_copy(bo, bo_hbm, local_sem.at[0])
    bo_out.start()
    halo_wait(gtile, gleft, gright, ghr, range(8))
    shifted(gtile, gleft, gright, xg, tuple(range(10)), True)
    weight_group((10, 11), (12, 13))
    weight_group((12, 13), ())
    feature_gradient((3, 2))
    first_sum(0)
    first_sum(1)
    feature_gradient((1, 0))
    fg_out = pltpu.make_async_copy(fg, fg_hbm, local_sem.at[1])
    fg_out.start()
    second_sum(0)
    first_sum(2)
    second_sum(1)
    first_sum(3)
    second_sum(2)
    second_sum(3)
    for q in range(4):
        for d in range(1, 8):
            third_copy(q, d).wait_recv()
        total = of[zlo, zhi, q]
        for d in range(7):
            total = total + r3[q, d].astype(F32)
        wg_ref[q] = total * (1.0 / 512.0)

    for present, copy in halo + ghalo:
        pl.when(present)(copy.wait_send)
    for i in range(5):
        x_copy(i).wait_send()
    for t in range(4):
        g_copy(t).wait_send()

    @pl.loop(0, PAIRS // 2)
    def _(i):
        for k in range(2):
            for d in (1, 2, 3):
                first_copy(2 * i + k, d, k == 0).wait_send()
                second_copy(2 * i + k, d, k == 1).wait_send()

    @pl.loop(0, 4)
    def _(q):
        for d in range(1, 8):
            third_copy(q, d).wait_send()
    bo_out.wait()
    fg_out.wait()


def finish(bo_in, fg_in, packed, bo_out, fg_out, wg_out, flat, sems):
    copies = [pltpu.make_async_copy(bo_in, bo_out, sems.at[0]), pltpu.make_async_copy(fg_in, fg_out, sems.at[1])]
    for copy in copies:
        copy.start()
    for q in range(4):
        flipped = packed[q].T
        for e in range(8):
            tap = 8 * q + 2 * (e % 4) + e // 4
            flat[tap * 16:tap * 16 + 16, :] = flipped[e * 16:e * 16 + 16, :]
    for k in range(16):
        wg_out[k] = flat[pl.ds(k, 32, stride=16), :].T[:, :27]
    for copy in copies:
        copy.wait()


def per_device(features, weights, cotangent):
    dma = pltpu.SemaphoreType.DMA
    anywhere = pl.BlockSpec(memory_space=pl.ANY)
    vmem = pl.BlockSpec(memory_space=pltpu.VMEM)
    block = jax.ShapeDtypeStruct((4, 8, 32, 256), BF)
    block_out, feature_grad, packed = pl.pallas_call(
        kernel,
        out_shape=(block, block, jax.ShapeDtypeStruct((4, 16, 128), F32)),
        in_specs=[anywhere] * 3,
        out_specs=(anywhere, anywhere, vmem),
        scratch_shapes=[
            pltpu.VMEM((9, 768, 256), BF), pltpu.VMEM((6, 768, 256), BF),
            pltpu.VMEM((4, 10, 64, 256), BF), pltpu.VMEM((4, 10, 64, 256), BF),
            pltpu.VMEM((3, 4, 320, 256), BF), pltpu.VMEM((3, 4, 320, 256), BF), pltpu.VMEM((3, 4, 320, 256), BF),
            pltpu.VMEM((4, 8, 32, 256), BF), pltpu.VMEM((4, 8, 32, 256), BF), pltpu.VMEM((4, 8, 32, 256), BF),
            pltpu.VMEM((4, 256, 256), F32), pltpu.VMEM((2, 128, 256), F32), pltpu.VMEM((4, 2, 128, 256), F32),
            pltpu.VMEM((8, 2, 16, 1024), BF), pltpu.VMEM((8, 16, 1024), BF),
            pltpu.VMEM((128, 256), BF), pltpu.VMEM((128, 256), BF),
            pltpu.VMEM((64, 256), BF), pltpu.VMEM((64, 256), BF), pltpu.VMEM((64, 256), BF), pltpu.VMEM((64, 256), BF),
            pltpu.VMEM((PAIRS, 4, 4, 32, 128), F32), pltpu.VMEM((PAIRS, 4, 4, 32, 128), BF),
            pltpu.VMEM((PAIRS, 3, 4, 32, 128), BF),
            pltpu.VMEM((PAIRS, 4, 32, 128), F32), pltpu.VMEM((PAIRS, 4, 32, 128), BF),
            pltpu.VMEM((PAIRS, 3, 32, 128), BF), pltpu.VMEM((PAIRS, 32, 128), F32),
            pltpu.VMEM((4, 2, 4, 16, 128), F32), pltpu.VMEM((4, 2, 4, 16, 128), BF), pltpu.VMEM((4, 7, 16, 128), BF),
            dma((3,)), dma((8,)), dma((8,)), dma((8,)), dma((8,)), dma((5,)), dma((5,)), dma((4,)), dma((4,)),
            dma((PAIRS, 3)), dma((PAIRS, 3)), dma((PAIRS, 3)), dma((PAIRS, 3)), dma((4, 7)), dma((4, 7)),
        ],
        compiler_params=pltpu.CompilerParams(collective_id=0, has_side_effects=True, vmem_limit_bytes=60 << 20),
        cost_estimate=pl.CostEstimate(flops=9_000_000_000, bytes_accessed=6_000_000, transcendentals=300_000),
        name="conv_block",
    )(features, weights.reshape(9, 768, 256), cotangent)
    block_out, feature_grad, grads = pl.pallas_call(
        finish,
        out_shape=(block, block, jax.ShapeDtypeStruct((16, 16, 27), F32)),
        in_specs=[vmem] * 3,
        out_specs=(anywhere, anywhere, vmem),
        scratch_shapes=[pltpu.VMEM((512, 16), F32), dma((2,))],
        name="finish",
    )(block_out, feature_grad, packed)
    return block_out, feature_grad, grads.transpose(2, 0, 1)


def solution(mesh):
    in_specs = (P(None, "ha", "wa", None), P(), P(None, "ha", "wa", None))
    out_specs = (P(None, "ha", "wa", None), P(None, "ha", "wa", None), P(None, "ha", "wa"))
    return jax.shard_map(
        per_device, mesh=mesh, in_specs=in_specs, out_specs=out_specs, check_vma=False
    )
```

profile of v0, /device:TPU:1, one launch (start us, length us, event | category | flops | bytes accessed | tf_op | source)
XLA Modules:
  0.0 51.2 jit_solution(9292708722026368961)
XLA Ops:
  0.6 47.6 %conv_block.1 = (bf16[4,8,32,256]{3,2,1,0:T(8,128)(2,1)}, bf16[4,8,32,256]{3,2,1,0:T(8,128)(2,1)}, f32[4,16,128]{2,1,0:T(8,128)}) custom-call(bf16[4,8,32,256]{3,2,1,0:T(8,128)(2,1)} %feat_hbm.1, bf16[9,768,256]{2,1,0:T(8,128)(2,1)} %bitcast.2, bf16[4,8,32,256]{3,2,1,0:T(8,128)(2,1)} %cot_hbm.1), custom_call_target="tpu_custom_call" | custom-call | flops 8999999488 | bytes 6000000 | tf_op jit(solution)/shard_map/conv_block/pallas_call | solution.py:430
  48.2 2.8 %finish.1 = (bf16[4,8,32,256]{3,2,1,0:T(8,128)(2,1)}, bf16[4,8,32,256]{3,2,1,0:T(8,128)(2,1)}, f32[16,16,27]{2,1,0:T(8,128)}) custom-call(bf16[4,8,32,256]{3,2,1,0:T(8,128)(2,1)} %get-tuple-element.9.bo_in, bf16[4,8,32,256]{3,2,1,0:T(8,128)(2,1)} %get-tuple-element.10.fg_in, f32[4,16,128]{2,1,0:T(8,128)} %get-tuple-element.11.packed), custom_call_target="tpu_custom_call" | custom-call | tf_op jit(solution)/shard_map/finish/pallas_call | solution.py:456
where the time goes:
time: 51.4 us; the launch traced here: 51.2 us
  Pallas kernels  50.4 us (98%)
  between operations  0.8 us (2%)
    pallas_call x1, Pallas kernels, per_device(): pl.pallas_call(kernel, out_shape=(block, block, jax.ShapeDtypeStruct((4,...  47.6 us
    pallas_call x1, Pallas kernels, per_device(): pl.pallas_call(finish, out_shape=(block, block, jax.ShapeDtypeStruct((16,...  2.84 us

commit v1 on v0

--- a/solution.py
+++ b/solution.py
@@ -29,7 +29,7 @@
     w_ref, wsum, tile, gtile, xc, xc2, xg, cot, bo, fg, acc_ref, fix_ref, hold, gt, gt2,
     cols, gcols, left, right, gleft, gright,
     part, partb, r1, s1, s1b, r2, s2, of, ob, r3,
-    local_sem, hs, hr, ghs, ghr, xcs, xcr, gts, gtr, s1s, s1r, s2s, s2r, s3s, s3r,
+    local_sem, hs, hr, ghr, xcs, xcr, gts, gtr, s1s, s1r, s2s, s2r, s3s, s3r,
 ):
     ha, wa = lax.axis_index("ha"), lax.axis_index("wa")
     x, zlo = ha // 4, ha % 4
@@ -150,9 +150,8 @@
     def x_copy(i):
         ref = (lambda b: (b.at[1, :, 32:288], b.at[0, :, 32:288], b.at[2, :, 32:288], b.at[:, :, 0:32], b.at[:, :, 288:320])[i])
         return pltpu.make_async_remote_copy(
-            src_ref=ref(xc), dst_ref=ref(xc2), send_sem=xcs.at[i], recv_sem=xcr.at[i], device_id=other, device_id_type=MESH)
-
-    x_copy(0).start()
+            src_ref=ref(xc), dst_ref=ref(xc2), send_sem=xcs, recv_sem=xcr, device_id=other, device_id_type=MESH)
+
     loads[1].wait()
 
     def forward(t, columns):
@@ -176,8 +175,8 @@
         acc_ref[t] = forward(t, (1,))
     halo_wait(tile, left, right, hr, (2, 3))
     shifted(tile, left, right, xc, middle, False)
-    x_copy(1).start()
-    x_copy(2).start()
+    for i in range(3):
+        x_copy(i).start()
     for t in range(4):
         acc_ref[t] += forward(t, (0, 2))
     halo_wait(tile, left, right, hr, (0, 1, 4, 5, 6, 7))
@@ -197,7 +196,7 @@
     def g_copy(t):
         return pltpu.make_async_remote_copy(
             src_ref=gt.at[:, 1 - core, :, t * 256:t * 256 + 256], dst_ref=gt2.at[:, :, t * 256:t * 256 + 256],
-            send_sem=gts.at[t], recv_sem=gtr.at[t], device_id=other, device_id_type=MESH)
+            send_sem=gts, recv_sem=gtr, device_id=other, device_id_type=MESH)
 
     for t in range(4):
         acc_ref[t, 0:32] += fix_ref[0, t * 32:t * 32 + 32]
@@ -239,22 +238,25 @@
                         part[p, i, j, zz * 16:zz * 16 + 16] = rows
                         partb[p, i, j, zz * 16:zz * 16 + 16] = rows.astype(BF)
 
+    def arrived(ref, sem):
+        pltpu.make_async_copy(ref, ref, sem).wait()
+
     def first_copy(p, d, by_y):
         return pltpu.make_async_remote_copy(
             src_ref=partb.at[p, ((y if by_y else x) + d) % 4], dst_ref=r1.at[p, d - 1],
-            send_sem=s1s.at[p, d - 1], recv_sem=s1r.at[p, d - 1],
+            send_sem=s1s, recv_sem=s1r.at[p // 4],
             device_id=device(dy=d) if by_y else device(dx=d), device_id_type=MESH)
 
-    def second_copy(p, d, by_y):
+    def second_copy(p, d, by_y, q):
         return pltpu.make_async_remote_copy(
             src_ref=s1b.at[p, ((y if by_y else x) + d) % 4], dst_ref=r2.at[p, d - 1],
-            send_sem=s2s.at[p, d - 1], recv_sem=s2r.at[p, d - 1],
+            send_sem=s2s, recv_sem=s2r.at[q],
             device_id=device(dy=d) if by_y else device(dx=d), device_id_type=MESH)
 
     def third_copy(q, d):
         nz = (z + d) % 8
         return pltpu.make_async_remote_copy(
-            src_ref=ob.at[nz % 4, nz // 4, q], dst_ref=r3.at[q, d - 1], send_sem=s3s.at[q, d - 1], recv_sem=s3r.at[q, d - 1],
+            src_ref=ob.at[nz % 4, nz // 4, q], dst_ref=r3.at[q, d - 1], send_sem=s3s, recv_sem=s3r.at[q],
             device_id=device(dz=d), device_id_type=MESH)
 
     def over_pairs(q, body):
@@ -279,20 +281,19 @@
         for p in done:
             store_pair(p, p % 2 == 0)
         for p in done:
-            for d in (2, 1, 3):
+            for d in (1, 3, 2):
                 first_copy(p, d, p % 2 == 0).start()
 
     def first_sum(q):
         def body(p, by_y):
-            for d in (1, 2, 3):
-                first_copy(p, d, by_y).wait_recv()
             total = part[p, y if by_y else x]
             for d in range(3):
                 total = total + r1[p, d].astype(F32)
             s1[p] = total
             s1b[p] = total.astype(BF)
-            for d in (2, 1, 3):
-                second_copy(p, d, not by_y).start()
+            for d in (1, 3, 2):
+                second_copy(p, d, not by_y, q).start()
+        arrived(r1.at[4 * q:min(4 * q + 4, PAIRS)], s1r.at[q])
         over_pairs(q, body)
 
     lane = iota((32, 128), 1)
@@ -304,12 +305,11 @@
 
     def second_sum(q):
         def body(p, by_y):
-            for d in (1, 2, 3):
-                second_copy(p, d, not by_y).wait_recv()
             total = s1[p, x if by_y else y]
             for d in range(3):
                 total = total + r2[p, d].astype(F32)
             s2[p] = total
+        arrived(r2.at[4 * q:min(4 * q + 4, PAIRS)], s2r.at[q])
         over_pairs(q, body)
         v = [s2[4 * q + i] if 4 * q + i < PAIRS else jnp.zeros((32, 128), F32) for i in range(4)]
         v[0], v[1] = exchange(v[0], v[1], 16)
@@ -323,32 +323,27 @@
         for d in (4, 3, 5, 2, 6, 1, 7):
             third_copy(q, d).start()
 
-    def feature_gradient(frames):
-        jobs = {}
-        for t in frames:
-            terms = [(t + 2 - a, a) for a in range(3) if t + 2 - a < 4] if t else [(2, 0), (1, 3), (0, 4)]
-            jobs[t] = [(f, a, b, c) for f, a in terms for b in range(3) for c in range(3)]
-        totals = dict.fromkeys(frames)
-        for i in range(max(len(job) for job in jobs.values())):
-            for t in frames:
-                if i < len(jobs[t]):
-                    f, a, b, c = jobs[t][i]
+    def feature_gradient(t):
+        terms = [(t + 2 - a, a) for a in range(3) if t + 2 - a < 4] if t else [(2, 0), (1, 3), (0, 4)]
+        total = None
+        for f, a in terms:
+            for b in range(3):
+                for c in range(3):
                     index = a * 3 + 2 - b if a < 3 else (a - 3) * 3 + 2 - b
                     weight = (w_ref if a < 3 else wsum)[index, (2 - c) * 256:(2 - c) * 256 + 256, :]
                     term = nt(xg[c, f, b * 32:b * 32 + 256, :], weight)
-                    totals[t] = term if totals[t] is None else totals[t] + term
-        for t in frames:
-            total = totals[t] + cot[t].reshape(256, 256).astype(F32)
-            fg[t] = total.astype(BF).reshape(8, 32, 256)
-
-    ghalo = halo_copies(gtile, gcols, gleft, gright, ghs, ghr)
+                    total = term if total is None else total + term
+        total = total + cot[t].reshape(256, 256).astype(F32)
+        fg[t] = total.astype(BF).reshape(8, 32, 256)
+
+    for present, copy in halo:
+        pl.when(present)(copy.wait_send)
+    ghalo = halo_copies(gtile, gcols, gleft, gright, hs, ghr)
     for i in (0, 1):
         pl.when(ghalo[i][0])(ghalo[i][1].start)
     own_terms(range(4))
-    for t in range(4):
-        g_copy(t).wait_recv()
-    for i in range(5):
-        x_copy(i).wait_recv()
+    arrived(gt2, gtr)
+    arrived(xc2, xcr)
     weight_group((), (0,))
     weight_group((0,), (1,))
     weight_group((1,), (2, 3))
@@ -365,10 +360,12 @@
     shifted(gtile, gleft, gright, xg, tuple(range(10)), True)
     weight_group((10, 11), (12, 13))
     weight_group((12, 13), ())
-    feature_gradient((3, 2))
+    feature_gradient(3)
+    feature_gradient(2)
     first_sum(0)
     first_sum(1)
-    feature_gradient((1, 0))
+    feature_gradient(1)
+    feature_gradient(0)
     fg_out = pltpu.make_async_copy(fg, fg_hbm, local_sem.at[1])
     fg_out.start()
     second_sum(0)
@@ -378,31 +375,19 @@
     second_sum(2)
     second_sum(3)
     for q in range(4):
-        for d in range(1, 8):
-            third_copy(q, d).wait_recv()
+        arrived(r3.at[q], s3r.at[q])
         total = of[zlo, zhi, q]
         for d in range(7):
             total = total + r3[q, d].astype(F32)
         wg_ref[q] = total * (1.0 / 512.0)
 
-    for present, copy in halo + ghalo:
+    for present, copy in ghalo:
         pl.when(present)(copy.wait_send)
-    for i in range(5):
-        x_copy(i).wait_send()
-    for t in range(4):
-        g_copy(t).wait_send()
-
-    @pl.loop(0, PAIRS // 2)
-    def _(i):
-        for k in range(2):
-            for d in (1, 2, 3):
-                first_copy(2 * i + k, d, k == 0).wait_send()
-                second_copy(2 * i + k, d, k == 1).wait_send()
-
-    @pl.loop(0, 4)
-    def _(q):
-        for d in range(1, 8):
-            third_copy(q, d).wait_send()
+    arrived(xc, xcs)
+    arrived(gt2, gts)
+    arrived(r1, s1s)
+    arrived(r2, s2s)
+    arrived(r3, s3s)
     bo_out.wait()
     fg_out.wait()
 
@@ -446,8 +431,8 @@
             pltpu.VMEM((PAIRS, 4, 32, 128), F32), pltpu.VMEM((PAIRS, 4, 32, 128), BF),
             pltpu.VMEM((PAIRS, 3, 32, 128), BF), pltpu.VMEM((PAIRS, 32, 128), F32),
             pltpu.VMEM((4, 2, 4, 16, 128), F32), pltpu.VMEM((4, 2, 4, 16, 128), BF), pltpu.VMEM((4, 7, 16, 128), BF),
-            dma((3,)), dma((8,)), dma((8,)), dma((8,)), dma((8,)), dma((5,)), dma((5,)), dma((4,)), dma((4,)),
-            dma((PAIRS, 3)), dma((PAIRS, 3)), dma((PAIRS, 3)), dma((PAIRS, 3)), dma((4, 7)), dma((4, 7)),
+            dma((3,)), dma((8,)), dma((8,)), dma((8,)), dma, dma, dma, dma,
+            dma, dma((4,)), dma, dma((4,)), dma, dma((4,)),
         ],
         compiler_params=pltpu.CompilerParams(collective_id=0, has_side_effects=True, vmem_limit_bytes=60 << 20),
         cost_estimate=pl.CostEstimate(flops=9_000_000_000, bytes_accessed=6_000_000, transcendentals=300_000),

time: 51.4 us -> 49.2 us (0.957)
  Pallas kernels: 50.4 us -> 48.3 us
    pallas_call x1, Pallas kernels: 47.6 us -> 45.5 us  [per_device(): pl.pallas_call(kernel, out_shape=(block, block, jax.ShapeDtypeStruct((4,...]
where the time goes in v1:
time: 49.2 us; the launch traced here: 49.1 us
  Pallas kernels  48.3 us (98%)
  between operations  0.8 us (2%)
    pallas_call x1, Pallas kernels, per_device(): pl.pallas_call(kernel, out_shape=(block, block, jax.ShapeDtypeStruct((4,...  45.5 us
    pallas_call x1, Pallas kernels, per_device(): pl.pallas_call(finish, out_shape=(block, block, jax.ShapeDtypeStruct((16,...  2.84 us

profile of v1, /device:TPU:1, one launch (start us, length us, event | category | flops | bytes accessed | tf_op | source)
XLA Modules:
  0.0 49.1 jit_solution(1623553019904176681)
XLA Ops:
  0.6 45.5 %conv_block.1 = (bf16[4,8,32,256]{3,2,1,0:T(8,128)(2,1)}, bf16[4,8,32,256]{3,2,1,0:T(8,128)(2,1)}, f32[4,16,128]{2,1,0:T(8,128)}) custom-call(bf16[4,8,32,256]{3,2,1,0:T(8,128)(2,1)} %feat_hbm.1, bf16[9,768,256]{2,1,0:T(8,128)(2,1)} %bitcast.2, bf16[4,8,32,256]{3,2,1,0:T(8,128)(2,1)} %cot_hbm.1), custom_call_target="tpu_custom_call" | custom-call | flops 8999999488 | bytes 6000000 | tf_op jit(solution)/shard_map/conv_block/pallas_call | solution.py:415
  46.1 2.8 %finish.1 = (bf16[4,8,32,256]{3,2,1,0:T(8,128)(2,1)}, bf16[4,8,32,256]{3,2,1,0:T(8,128)(2,1)}, f32[16,16,27]{2,1,0:T(8,128)}) custom-call(bf16[4,8,32,256]{3,2,1,0:T(8,128)(2,1)} %get-tuple-element.9.bo_in, bf16[4,8,32,256]{3,2,1,0:T(8,128)(2,1)} %get-tuple-element.10.fg_in, f32[4,16,128]{2,1,0:T(8,128)} %get-tuple-element.11.packed), custom_call_target="tpu_custom_call" | custom-call | tf_op jit(solution)/shard_map/finish/pallas_call | solution.py:441

commit v2 on v1

--- a/solution.py
+++ b/solution.py
@@ -356,24 +356,22 @@
     weight_group((8, 9), (10, 11))
     bo_out = pltpu.make_async_copy(bo, bo_hbm, local_sem.at[0])
     bo_out.start()
+    weight_group((10, 11), (12, 13))
+    weight_group((12, 13), ())
     halo_wait(gtile, gleft, gright, ghr, range(8))
     shifted(gtile, gleft, gright, xg, tuple(range(10)), True)
-    weight_group((10, 11), (12, 13))
-    weight_group((12, 13), ())
     feature_gradient(3)
     feature_gradient(2)
-    first_sum(0)
-    first_sum(1)
+    for q in range(4):
+        first_sum(q)
+    second_sum(0)
+    second_sum(1)
     feature_gradient(1)
+    second_sum(2)
+    second_sum(3)
     feature_gradient(0)
     fg_out = pltpu.make_async_copy(fg, fg_hbm, local_sem.at[1])
     fg_out.start()
-    second_sum(0)
-    first_sum(2)
-    second_sum(1)
-    first_sum(3)
-    second_sum(2)
-    second_sum(3)
     for q in range(4):
         arrived(r3.at[q], s3r.at[q])
         total = of[zlo, zhi, q]

time: 49.2 us -> 48.9 us (level)
  no operation moved by 1% of the time
where the time goes in v2:
time: 48.9 us; the launch traced here: 48.8 us
  Pallas kernels  48 us (98%)
  between operations  0.8 us (2%)
    pallas_call x1, Pallas kernels, per_device(): pl.pallas_call(kernel, out_shape=(block, block, jax.ShapeDtypeStruct((4,...  45.2 us
    pallas_call x1, Pallas kernels, per_device(): pl.pallas_call(finish, out_shape=(block, block, jax.ShapeDtypeStruct((16,...  2.84 us

profile of v2, /device:TPU:1, one launch (start us, length us, event | category | flops | bytes accessed | tf_op | source)
XLA Modules:
  0.0 48.8 jit_solution(10330515141587747659)
XLA Ops:
  0.6 45.2 %conv_block.1 = (bf16[4,8,32,256]{3,2,1,0:T(8,128)(2,1)}, bf16[4,8,32,256]{3,2,1,0:T(8,128)(2,1)}, f32[4,16,128]{2,1,0:T(8,128)}) custom-call(bf16[4,8,32,256]{3,2,1,0:T(8,128)(2,1)} %feat_hbm.1, bf16[9,768,256]{2,1,0:T(8,128)(2,1)} %bitcast.2, bf16[4,8,32,256]{3,2,1,0:T(8,128)(2,1)} %cot_hbm.1), custom_call_target="tpu_custom_call" | custom-call | flops 8999999488 | bytes 6000000 | tf_op jit(solution)/shard_map/conv_block/pallas_call | solution.py:413
  45.8 2.8 %finish.1 = (bf16[4,8,32,256]{3,2,1,0:T(8,128)(2,1)}, bf16[4,8,32,256]{3,2,1,0:T(8,128)(2,1)}, f32[16,16,27]{2,1,0:T(8,128)}) custom-call(bf16[4,8,32,256]{3,2,1,0:T(8,128)(2,1)} %get-tuple-element.9.bo_in, bf16[4,8,32,256]{3,2,1,0:T(8,128)(2,1)} %get-tuple-element.10.fg_in, f32[4,16,128]{2,1,0:T(8,128)} %get-tuple-element.11.packed), custom_call_target="tpu_custom_call" | custom-call | tf_op jit(solution)/shard_map/finish/pallas_call | solution.py:439

commit v3 on v2

--- a/solution.py
+++ b/solution.py
@@ -141,7 +141,7 @@
     cols[...] = mm(select, tile[:, 1:9, 16:48, :].reshape(1024, 256)).astype(BF)
     pl.semaphore_wait(barrier, count)
     halo = halo_copies(tile, cols, left, right, hs, hr)
-    for i in (2, 3, 0, 1, 4, 5, 6, 7):
+    for i in (2, 3, 4, 5, 6, 7, 0, 1):
         pl.when(halo[i][0])(halo[i][1].start)
     for t in range(4):
         for r in middle:
@@ -203,8 +203,6 @@
         acc_ref[t, 224:256] += fix_ref[1, t * 32:t * 32 + 32]
         acc = acc_ref[t]
         logistic = jax.nn.sigmoid(acc)
-        own = tile[t, 1:9, 16:48, :].reshape(256, 256).astype(F32)
-        bo[t] = (own + acc * logistic).astype(BF).reshape(8, 32, 256)
         grad = cot[t].reshape(256, 256).astype(F32) * logistic * (1.0 + acc * (1.0 - logistic))
         grad = grad.astype(BF)
         gtile[t, 1:9, 16:48, :] = grad.reshape(8, 32, 256)
@@ -345,7 +343,8 @@
     arrived(gt2, gtr)
     arrived(xc2, xcr)
     weight_group((), (0,))
-    weight_group((0,), (1,))
+    weight_group((0,), ())
+    weight_group((), (1,))
     weight_group((1,), (2, 3))
     gcols[...] = mm(select, gtile[:, 1:9, 16:48, :].reshape(1024, 256)).astype(BF)
     for i in range(2, 8):
@@ -354,8 +353,6 @@
     weight_group((4, 5), (6, 7))
     weight_group((6, 7), (8, 9))
     weight_group((8, 9), (10, 11))
-    bo_out = pltpu.make_async_copy(bo, bo_hbm, local_sem.at[0])
-    bo_out.start()
     weight_group((10, 11), (12, 13))
     weight_group((12, 13), ())
     halo_wait(gtile, gleft, gright, ghr, range(8))
@@ -369,6 +366,12 @@
     feature_gradient(1)
     second_sum(2)
     second_sum(3)
+    for t in range(4):
+        acc = acc_ref[t]
+        own = tile[t, 1:9, 16:48, :].reshape(256, 256).astype(F32)
+        bo[t] = (own + acc * jax.nn.sigmoid(acc)).astype(BF).reshape(8, 32, 256)
+    bo_out = pltpu.make_async_copy(bo, bo_hbm, local_sem.at[0])
+    bo_out.start()
     feature_gradient(0)
     fg_out = pltpu.make_async_copy(fg, fg_hbm, local_sem.at[1])
     fg_out.start()

time: 48.9 us -> 48.8 us (level)
  no operation moved by 1% of the time
where the time goes in v3:
time: 48.8 us; the launch traced here: 48.7 us
  Pallas kernels  47.9 us (98%)
  between operations  0.8 us (2%)
    pallas_call x1, Pallas kernels, per_device(): pl.pallas_call(kernel, out_shape=(block, block, jax.ShapeDtypeStruct((4,...  45 us
    pallas_call x1, Pallas kernels, per_device(): pl.pallas_call(finish, out_shape=(block, block, jax.ShapeDtypeStruct((16,...  2.84 us

profile of v3, /device:TPU:1, one launch (start us, length us, event | category | flops | bytes accessed | tf_op | source)
XLA Modules:
  0.0 48.7 jit_solution(5905099962794910497)
XLA Ops:
  0.6 45.0 %conv_block.1 = (bf16[4,8,32,256]{3,2,1,0:T(8,128)(2,1)}, bf16[4,8,32,256]{3,2,1,0:T(8,128)(2,1)}, f32[4,16,128]{2,1,0:T(8,128)}) custom-call(bf16[4,8,32,256]{3,2,1,0:T(8,128)(2,1)} %feat_hbm.1, bf16[9,768,256]{2,1,0:T(8,128)(2,1)} %bitcast.2, bf16[4,8,32,256]{3,2,1,0:T(8,128)(2,1)} %cot_hbm.1), custom_call_target="tpu_custom_call" | custom-call | flops 8999999488 | bytes 6000000 | tf_op jit(solution)/shard_map/conv_block/pallas_call | solution.py:416
  45.7 2.8 %finish.1 = (bf16[4,8,32,256]{3,2,1,0:T(8,128)(2,1)}, bf16[4,8,32,256]{3,2,1,0:T(8,128)(2,1)}, f32[16,16,27]{2,1,0:T(8,128)}) custom-call(bf16[4,8,32,256]{3,2,1,0:T(8,128)(2,1)} %get-tuple-element.9.bo_in, bf16[4,8,32,256]{3,2,1,0:T(8,128)(2,1)} %get-tuple-element.10.fg_in, f32[4,16,128]{2,1,0:T(8,128)} %get-tuple-element.11.packed), custom_call_target="tpu_custom_call" | custom-call | tf_op jit(solution)/shard_map/finish/pallas_call | solution.py:442
